TPU v7x, 512 devices: a whole 4x4x16 slice. The times are simulated.
512 devices in a mesh: dp: 16 (over z_hi, x), lat: 32 (over y, z_lo, core).
Axes of the slice: x: 4, y: 4, z: 16 (z_hi: 4, z_lo: 4; z = z_hi * 4 + z_lo), core: 2. Of those that a mesh axis runs over, the one named last changes fastest.
Arguments:
- states: bfloat16 [16, 128, 128, 128], P('dp', 'lat'), may hold values from -6 to 6
- basis_table: bfloat16 [128, 25, 9, 5], replicated, may hold values from -1.1953125 to 1.1953125
- offsets: int32 [128], replicated, may hold values from -12 to -8, as said below
- widths: int32 [128], replicated, may hold values from 21 to 25, as said below
- mixing: bfloat16 [9, 128, 128], replicated, may hold values from -0.1875 to 0.1875
- cotangent: bfloat16 [16, 128, 128, 128], P('dp', 'lat'), may hold values from -6 to 6
Outputs:
- output: bfloat16 [16, 128, 128, 128], P('dp', 'lat')
- grad_states: bfloat16 [16, 128, 128, 128], P('dp', 'lat')
- grad_mixing: float32 [9, 128, 128], replicated
Inputs may be any that keep to these rules, and one draw needn't show every extreme that they name: The support of every output latitude o contains o itself and lies within latitudes o - 12 to o + 12, so offsets[o] is at most 13 - widths[o]. widths is 25 at the two pole latitudes 0 and 127.
All inputs are finite; a program needn't handle non-finite values.
Results may differ from a plain program's by a relative error of at most 0.0049.
Values may be sent and summed in bfloat16 or wider, within the bound.
No kernel may reach another device: no remote copies, remote signals or barrier semaphores. Data moves between devices by JAX's collectives and lax.ppermute only.
A program may use at most 64 MiB of HBM per device.

v0:
```python
import math
import jax
import jax.numpy as jnp
from jax import lax
from jax.sharding import PartitionSpec as P

TAPS = 5
HALO = 12


def shifted(x, axis, by):
    count = lax.axis_size(axis)
    pairs = [(i, i + by) for i in range(count) if 0 <= i + by < count]
    return lax.ppermute(x, axis, pairs)


def band_matrix(table_rows, offsets, widths, ext_rows, offset_base):
    out_rows = offsets.shape[0]
    support = table_rows.shape[1]
    slot_ids = jnp.arange(support, dtype=jnp.int32)
    target = (
        jnp.arange(out_rows, dtype=jnp.int32)[:, None]
        + offset_base
        + offsets[:, None]
        + slot_ids[None, :]
    )
    column = jnp.arange(ext_rows, dtype=jnp.int32)
    matches = (target[:, :, None] == column[None, None, :]) & (
        slot_ids[None, :, None] < widths[:, None, None]
    )
    return jnp.einsum(
        "qskt,qse->ktqe",
        table_rows,
        matches.astype(jnp.bfloat16),
        preferred_element_type=jnp.float32,
    ).astype(jnp.bfloat16)


def halo_rows(stacked, axis_rows):
    band_rows = stacked.shape[axis_rows]
    hop_count = -(-HALO // band_rows)
    above = []
    for distance in range(hop_count, 0, -1):
        row_count = min(band_rows, HALO - (distance - 1) * band_rows)
        piece = stacked
        above.append(shifted(piece, "lat", distance))
    below = []
    for distance in range(1, hop_count + 1):
        row_count = min(band_rows, HALO - (distance - 1) * band_rows)
        piece = stacked
        below.append(shifted(piece, "lat", -distance))
    return jnp.concatenate(above + [stacked] + below, axis=axis_rows)


def adjoint_rows(matrix, grad_filtered, half_taps):
    total = None
    for tap_index in range(TAPS):
        term = jnp.einsum(
            "kqe,bkqlc->belc",
            matrix[:, tap_index],
            grad_filtered,
            preferred_element_type=jnp.float32,
        )
        term = jnp.roll(term, tap_index - half_taps, axis=2)
        total = term if total is None else total + term
    return total


def shards(states, basis_table, offsets, widths, mixing, cotangent):
    band_rows = states.shape[1]
    half_taps = TAPS // 2
    ext_rows = band_rows + 2 * HALO
    first_row = lax.axis_index("lat") * band_rows
    table_rows = lax.dynamic_slice_in_dim(basis_table, first_row, band_rows, 0)
    own_offsets = lax.dynamic_slice_in_dim(offsets, first_row, band_rows, 0)
    own_widths = lax.dynamic_slice_in_dim(widths, first_row, band_rows, 0)
    both_ext = halo_rows(jnp.stack((states, cotangent)), 2)
    states_ext = both_ext[0]
    cot_ext = both_ext[1]
    forward_matrix = band_matrix(table_rows, own_offsets, own_widths, ext_rows, HALO)
    rolled = jnp.stack(
        [jnp.roll(states_ext, half_taps - tap_index, axis=2) for tap_index in range(TAPS)], axis=1
    )
    filtered = jnp.einsum(
        "ktqe,btelc->bkqlc", forward_matrix, rolled, preferred_element_type=jnp.float32
    ).astype(jnp.bfloat16)
    output = jnp.einsum(
        "bkqlc,kcd->bqld", filtered, mixing, preferred_element_type=jnp.float32
    ).astype(jnp.bfloat16)
    grad_ext = jnp.einsum(
        "bqld,kcd->bkqlc", cot_ext, mixing, preferred_element_type=jnp.float32
    ).astype(jnp.bfloat16)
    table_pad = jnp.pad(basis_table, ((HALO, HALO), (0, 0), (0, 0), (0, 0)))
    offset_pad = jnp.pad(offsets, ((HALO, HALO),))
    width_pad = jnp.pad(widths, ((HALO, HALO),))
    adjoint_matrix = band_matrix(
        lax.dynamic_slice_in_dim(table_pad, first_row, ext_rows, 0),
        lax.dynamic_slice_in_dim(offset_pad, first_row, ext_rows, 0),
        lax.dynamic_slice_in_dim(width_pad, first_row, ext_rows, 0),
        band_rows,
        -HALO,
    )
    grad_states = adjoint_rows(adjoint_matrix, grad_ext, half_taps).astype(jnp.bfloat16)
    grad_local = jnp.einsum(
        "bkqlc,bqld->kcd", filtered, cotangent, preferred_element_type=jnp.float32
    )
    cell_count = (
        states.shape[0] * lax.axis_size("dp") * band_rows * lax.axis_size("lat") * states.shape[2]
    )
    grad_scale = 1.0 / math.sqrt(cell_count)
    grad_mixing = lax.psum(grad_local, ("dp", "lat")) * grad_scale
    return (output, grad_states, grad_mixing)


def solution(mesh):
    in_specs = (P("dp", "lat", None, None), P(), P(), P(), P(), P("dp", "lat", None, None))
    out_specs = (P("dp", "lat", None, None), P("dp", "lat", None, None), P())
    return jax.shard_map(shards, mesh=mesh, in_specs=in_specs, out_specs=out_specs, check_vma=False)
```

profile of v0, /device:TPU:1, one launch (start us, length us, event | category | flops | bytes accessed | tf_op | source)
XLA Modules:
  0.0 562.9 jit_solution(4812192866766922505)
XLA Ops:
  7.2 0.0 copy-start
  7.2 0.0 copy-start.9
  7.2 0.0 copy-start.2
  7.2 0.0 all-reduce.5.cloned.1.call-start
  7.2 1.3 copy_bitcast_fusion
  8.5 0.2 pad_maximum_fusion
  8.7 7.0 %collective-permute-start = (bf16[2,1,4,128,128]{4,2,3,1,0:T(4,128)(2,1)S(1)}, bf16[2,1,4,128,128]{4,2,3,1,0:T(4,128)(2,1)}, u32[]{:S(2)}, u32[]{:S(2)}) collective-permute-start(bf16[2,1,4,128,128]{4,2,3,1,0:T(4,128)(2,1)S(1)} %pad_maximum_fusion), channel_id=1, source_target_pairs={{0,3},{1,4},{2,5},{3,6},{4,7},{5,8},{6,9},{7,10},{8,11},{9,12},{10... | collective-permute-start | bytes 786440 | tf_op jit(solution)/shard_map/ppermute | solution.py:14
  15.7 3.6 collective-permute-start.1
  19.2 1.9 collective-permute-start.2
  21.2 3.1 collective-permute-start.3
  24.3 1.3 collective-permute-start.4
  25.6 0.8 pad_dynamic-slice_fusion.2
  26.3 0.7 iota_add_fusion
  27.0 0.1 iota_compare_fusion.2
  27.1 5.5 copy.17
  32.6 0.7 dynamic_slice.19
  33.4 0.6 iota_compare_fusion.3
  33.9 2.0 fusion.53
  35.9 0.2 constant_dynamic-slice_fusion
  36.1 0.1 slice_bitcast_fusion.4
  36.1 0.0 collective-permute-done
  36.2 1.3 collective-permute-start.5
  37.5 0.1 dynamic-slice_add_fusion
  37.5 0.7 copy.21
  38.3 0.1 copy.25
  38.4 0.1 copy.19
  38.5 0.1 copy.27
  38.6 0.1 copy.23
  38.8 0.6 copy.31
  39.4 0.1 iota_add_fusion.1
  39.5 0.0 collective-permute-done.1
  39.5 0.0 collective-permute-done.2
  39.5 0.0 collective-permute-done.3
  39.5 0.0 collective-permute-done.4
  39.5 10.8 %collective-permute-done.5 = bf16[2,1,4,128,128]{4,2,3,1,0:T(4,128)(2,1)S(1)} collective-permute-done((bf16[2,1,4,128,128]{4,2,3,1,0:T(4,128)(2,1)S(1)}, bf16[2,1,4,128,128]{4,2,3,1,0:T(4,128)(2,1)S(1)}, u32[]{:S(2)}, u32[]{:S(2)}) %collective-permute-start.5) | collective-permute-done | bytes 262176 | tf_op jit(solution)/shard_map/ppermute | solution.py:14
  50.2 6.7 %concatenate.51 = bf16[2,1,28,128,128]{4,2,3,1,0:T(8,128)(2,1)S(1)} concatenate(bf16[2,1,4,128,128]{4,2,3,1,0:T(4,128)(2,1)} %collective-permute-done, bf16[2,1,4,128,128]{4,2,3,1,0:T(4,128)(2,1)} %collective-permute-done.1, bf16[2,1,4,128,128]{4,2,3,1,0:T(4,128)(2,1)} %collective-permute-done.2, bf16[2,1,4,128,128]{4,2,3,1,0:T(4,128)(2,1)S(1)} %pad_maximum_fusion, ...), dimensions={2} | concatenate | bytes 3670016 | tf_op jit(solution)/shard_map/concatenate | solution.py:52
  57.0 0.4 slice_bitcast_fusion
  57.3 2.3 convert_bitcast_fusion
  59.7 0.0 copy-start.1
  59.7 4.5 fusion.20
  64.2 4.4 fusion.32
  68.6 4.6 fusion.23
  73.2 4.4 fusion.29
  77.6 0.8 slice.127
  78.4 0.3 fusion.87
  78.7 0.3 fusion.89
  79.0 0.0 copy-start.10
  79.0 1.2 fusion.58
  80.2 1.2 fusion.59
  81.4 1.2 bitcast_dynamic-update-slice_fusion
  82.7 1.2 fusion.60
  83.9 1.2 fusion.61
  85.1 0.0 slice-start.3
  85.2 0.0 slice-start.4
  85.2 0.0 slice-start.5
  85.2 0.0 slice-start.6
  85.2 3.7 fusion.14
  88.9 2.5 convolution_bitcast_fusion
  91.4 0.0 all-reduce.5.cloned.1.call-update
  91.5 7.8 %fusion.50 = bf16[1,4,128,128]{3,1,2,0:T(4,128)(2,1)S(1)} fusion(bf16[9,28,128,128]{3,2,0,1:T(8,128)(2,1)} %copy-done.1, f32[1,4,2,128]{3,1,2,0:T(4,128)S(1)} %slice-done.1, f32[1,4,126,128]{3,1,2,0:T(4,128)S(1)} %slice-done, f32[1,4,1,128]{3,1,2,0:T(4,128)S(1)} %slice-done.5, f32[1,4,127,128]{3,1,2,0:T(4,128)S(1)} %slice-done.4, ...), kind=kOutput, calls=%fused_computation.31 | convolution fusion | flops 33619968 | bytes 9439200 | tf_op jit(solution)/shard_map/kqe,bkqlc->belc/dot_general | solution.py:58
  99.3 0.7 copy.29
  100.0 1.6 fusion.54
  101.5 452.6 %all-reduce.5.cloned.1.call-done = f32[9,128,128]{2,1,0:T(8,128)} async-done(((f32[9,128,128]{2,1,0:T(8,128)}), f32[9,128,128]{2,1,0:T(8,128)}) %all-reduce.5.cloned.1.call-update) | async-done | bytes 589840 | tf_op jit(solution)/shard_map/psum | solution.py:111
  554.1 1.9 broadcast_multiply_fusion
  (29 shorter events, 0.1 us)
Async XLA Ops:
  7.2 50.2 %copy-start = (bf16[9,128,128]{2,1,0:T(8,128)(2,1)S(1)}, bf16[9,128,128]{2,1,0:T(8,128)(2,1)}, u32[]{:S(2)}) copy-start(bf16[9,128,128]{2,1,0:T(8,128)(2,1)} %param.10) | copy-start | bytes 884740
  7.2 30.3 %copy-start.9 = (s32[128]{0:T(128)S(1)}, s32[128]{0:T(128)}, u32[]{:S(2)}) copy-start(s32[128]{0:T(128)} %param.8) | copy-start | bytes 1540
  7.2 28.7 %copy-start.2 = (bf16[128,25,9,5]{0,1,3,2:T(8,128)(2,1)S(1)}, bf16[128,25,9,5]{0,1,3,2:T(8,128)(2,1)}, u32[]{:S(2)}) copy-start(bf16[128,25,9,5]{0,1,3,2:T(8,128)(2,1)} %param.7) | copy-start | bytes 864004
  7.2 546.9 %all-reduce.5.cloned.1.call-start = ((), (), s32[]{:S(2)}) async-start(), calls=%async_computation | async-start | bytes 1179648 | tf_op jit(solution)/shard_map/psum | solution.py:111
  8.7 27.4 %collective-permute-start = (bf16[2,1,4,128,128]{4,2,3,1,0:T(4,128)(2,1)S(1)}, bf16[2,1,4,128,128]{4,2,3,1,0:T(4,128)(2,1)}, u32[]{:S(2)}, u32[]{:S(2)}) collective-permute-start(bf16[2,1,4,128,128]{4,2,3,1,0:T(4,128)(2,1)S(1)} %pad_maximum_fusion), channel_id=1, source_target_pairs={{0,3},{1,4},{2,5},{3,6},{4,7},{5,8},{6,9},{7,10},{8,11},{9,12},{10... | collective-permute-start | bytes 786440 | tf_op jit(solution)/shard_map/ppermute | solution.py:14
  15.7 23.8 %collective-permute-start.1 = (bf16[2,1,4,128,128]{4,2,3,1,0:T(4,128)(2,1)S(1)}, bf16[2,1,4,128,128]{4,2,3,1,0:T(4,128)(2,1)}, u32[]{:S(2)}, u32[]{:S(2)}) collective-permute-start(bf16[2,1,4,128,128]{4,2,3,1,0:T(4,128)(2,1)S(1)} %pad_maximum_fusion), channel_id=1, source_target_pairs={{0,2},{1,3},{2,4},{3,5},{4,6},{5,7},{6,8},{7,9},{8,10},{9,11},{10,... | collective-permute-start | bytes 786440 | tf_op jit(solution)/shard_map/ppermute | solution.py:14
  19.2 20.2 %collective-permute-start.2 = (bf16[2,1,4,128,128]{4,2,3,1,0:T(4,128)(2,1)S(1)}, bf16[2,1,4,128,128]{4,2,3,1,0:T(4,128)(2,1)}, u32[]{:S(2)}, u32[]{:S(2)}) collective-permute-start(bf16[2,1,4,128,128]{4,2,3,1,0:T(4,128)(2,1)S(1)} %pad_maximum_fusion), channel_id=1, source_target_pairs={{0,1},{1,2},{2,3},{3,4},{4,5},{5,6},{6,7},{7,8},{8,9},{9,10},{10,1... | collective-permute-start | bytes 786440 | tf_op jit(solution)/shard_map/ppermute | solution.py:14
  21.2 18.3 %collective-permute-start.3 = (bf16[2,1,4,128,128]{4,2,3,1,0:T(4,128)(2,1)S(1)}, bf16[2,1,4,128,128]{4,2,3,1,0:T(4,128)(2,1)}, u32[]{:S(2)}, u32[]{:S(2)}) collective-permute-start(bf16[2,1,4,128,128]{4,2,3,1,0:T(4,128)(2,1)S(1)} %pad_maximum_fusion), channel_id=1, source_target_pairs={{1,0},{2,1},{3,2},{4,3},{5,4},{6,5},{7,6},{8,7},{9,8},{10,9},{11,1... | collective-permute-start | bytes 786440 | tf_op jit(solution)/shard_map/ppermute | solution.py:14
  24.3 15.2 %collective-permute-start.4 = (bf16[2,1,4,128,128]{4,2,3,1,0:T(4,128)(2,1)S(1)}, bf16[2,1,4,128,128]{4,2,3,1,0:T(4,128)(2,1)}, u32[]{:S(2)}, u32[]{:S(2)}) collective-permute-start(bf16[2,1,4,128,128]{4,2,3,1,0:T(4,128)(2,1)S(1)} %pad_maximum_fusion), channel_id=1, source_target_pairs={{2,0},{3,1},{4,2},{5,3},{6,4},{7,5},{8,6},{9,7},{10,8},{11,9},{12,... | collective-permute-start | bytes 786440 | tf_op jit(solution)/shard_map/ppermute | solution.py:14
  36.2 14.1 %collective-permute-start.5 = (bf16[2,1,4,128,128]{4,2,3,1,0:T(4,128)(2,1)S(1)}, bf16[2,1,4,128,128]{4,2,3,1,0:T(4,128)(2,1)S(1)}, u32[]{:S(2)}, u32[]{:S(2)}) collective-permute-start(bf16[2,1,4,128,128]{4,2,3,1,0:T(4,128)(2,1)S(1)} %pad_maximum_fusion), channel_id=1, source_target_pairs={{3,0},{4,1},{5,2},{6,3},{7,4},{8,5},{9,6},{10,7},{11,8},{12,9},{13... | collective-permute-start | bytes 786440 | tf_op jit(solution)/shard_map/ppermute | solution.py:14
  59.7 13.6 %copy-start.1 = (bf16[9,28,128,128]{3,2,0,1:T(8,128)(2,1)}, bf16[9,28,128,128]{3,2,0,1:T(8,128)(2,1)S(1)}, u32[]{:S(2)}) copy-start(bf16[9,28,128,128]{3,2,0,1:T(8,128)(2,1)S(1)} %convert_bitcast_fusion) | copy-start | bytes 24772612
  64.2 4.4 copy-start.4
  64.2 4.4 copy-start.8
  68.6 4.6 copy-start.5
  73.2 4.4 copy-start.6
  77.6 2.6 copy-start.7
  79.0 6.1 %copy-start.10 = (pred[4,25]{1,0:T(4,128)(4,1)S(1)}, pred[4,25]{1,0:T(4,128)(4,1)}, u32[]{:S(2)}) copy-start(pred[4,25]{1,0:T(4,128)(4,1)} %iota_compare_fusion.3) | copy-start | bytes 304
  83.9 4.9 copy-start.3
  85.1 6.3 %slice-start = ((f32[1,4,128,128]{3,1,2,0:T(4,128)}), f32[1,4,126,128]{3,1,2,0:T(4,128)S(1)}, s32[]{:S(2)}) async-start(f32[1,4,128,128]{3,1,2,0:T(4,128)} %copy-done.4), calls=%async_computation.1 | async-start | bytes 516096 | tf_op jit(solution)/shard_map/jit(_roll_static)/slice | solution.py:64
  85.1 6.3 %slice-start.1 = ((f32[1,4,128,128]{3,1,2,0:T(4,128)}), f32[1,4,2,128]{3,1,2,0:T(4,128)S(1)}, s32[]{:S(2)}) async-start(f32[1,4,128,128]{3,1,2,0:T(4,128)} %copy-done.4), calls=%async_computation.2 | async-start | bytes 8192 | tf_op jit(solution)/shard_map/jit(_roll_static)/slice | solution.py:64
  85.1 6.3 %slice-start.2 = ((f32[1,4,128,128]{3,1,2,0:T(4,128)}), f32[1,4,126,128]{3,1,2,0:T(4,128)S(1)}, s32[]{:S(2)}) async-start(f32[1,4,128,128]{3,1,2,0:T(4,128)} %copy-done.5), calls=%async_computation.3 | async-start | bytes 516096 | tf_op jit(solution)/shard_map/jit(_roll_static)/slice | solution.py:64
  85.1 6.3 %slice-start.3 = ((f32[1,4,128,128]{3,1,2,0:T(4,128)}), f32[1,4,2,128]{3,1,2,0:T(4,128)S(1)}, s32[]{:S(2)}) async-start(f32[1,4,128,128]{3,1,2,0:T(4,128)} %copy-done.5), calls=%async_computation.4 | async-start | bytes 8192 | tf_op jit(solution)/shard_map/jit(_roll_static)/slice | solution.py:64
  85.2 6.3 %slice-start.4 = ((f32[1,4,128,128]{3,1,2,0:T(4,128)}), f32[1,4,127,128]{3,1,2,0:T(4,128)S(1)}, s32[]{:S(2)}) async-start(f32[1,4,128,128]{3,1,2,0:T(4,128)} %copy-done.6), calls=%async_computation.5 | async-start | bytes 520192 | tf_op jit(solution)/shard_map/jit(_roll_static)/slice | solution.py:64
  85.2 6.3 %slice-start.5 = ((f32[1,4,128,128]{3,1,2,0:T(4,128)}), f32[1,4,1,128]{3,1,2,0:T(4,128)S(1)}, s32[]{:S(2)}) async-start(f32[1,4,128,128]{3,1,2,0:T(4,128)} %copy-done.6), calls=%async_computation.6 | async-start | bytes 4096 | tf_op jit(solution)/shard_map/jit(_roll_static)/slice | solution.py:64
  85.2 6.3 %slice-start.6 = ((f32[1,4,128,128]{3,1,2,0:T(4,128)}), f32[1,4,1,128]{3,1,2,0:T(4,128)S(1)}, s32[]{:S(2)}) async-start(f32[1,4,128,128]{3,1,2,0:T(4,128)} %copy-done.7), calls=%async_computation.7 | async-start | bytes 4096 | tf_op jit(solution)/shard_map/jit(_roll_static)/slice | solution.py:64
Sparse Core Ops, SparseCore 0:
  91.6 462.5 all-reduce.4
where the time goes:
time: 564 us; the launch traced here: 563 us
  waiting for transfers between devices  463 us (82%)
  matrix products  37.7 us (7%)
  local copies, waits for them, and re-layouts  20 us (4%)
  starting transfers between devices  18.2 us (3%)
  between operations  14.4 us (3%)
  other arithmetic  9.21 us (2%)
    psum x1, waiting for transfers between devices, shards(): grad_mixing = lax.psum(grad_local, ('dp', 'lat')) * grad_scale  453 us
    dot_general x5, matrix products, adjoint_rows(): jnp.einsum('kqe,bkqlc->belc', matrix[:, tap_index], grad_filtered, prefer...  25.7 us
    ppermute x6, starting transfers between devices, shifted(): return lax.ppermute(x, axis, pairs)  18.1 us
  transfers between devices with their start and end apart: 7, of which 2 were waited for; matrix products, arithmetic and copies ran while one was open for 4% of the time, Pallas kernels for 0%

commit v1 on v0

--- a/solution.py
+++ b/solution.py
@@ -108,7 +108,7 @@
         states.shape[0] * lax.axis_size("dp") * band_rows * lax.axis_size("lat") * states.shape[2]
     )
     grad_scale = 1.0 / math.sqrt(cell_count)
-    grad_mixing = lax.psum(grad_local, ("dp", "lat")) * grad_scale
+    grad_mixing = lax.psum(lax.psum(grad_local, "lat"), "dp") * grad_scale
     return (output, grad_states, grad_mixing)
 
 

time: 564 us -> 584 us (1.035); the launches traced: 563 us -> 573 us
  waiting for transfers between devices: 463 us -> 471 us
    psum x1 -> x2, waiting for transfers between devices: 453 us -> 460 us  [shards(): grad_mixing = lax.psum(lax.psum(grad_local, 'lat'), 'dp') * grad_scale]
  transfers between devices with their start and end apart: 7 -> 8, of which waited for: 2 -> 3; matrix products, arithmetic and copies ran while one was open for 4% -> 5% of each run, Pallas kernels for 0% -> 0%
where the time goes in v1:
time: 584 us; the launch traced here: 573 us
  waiting for transfers between devices  471 us (81%)
  matrix products  40.7 us (7%)
  local copies, waits for them, and re-layouts  19.2 us (3%)
  starting transfers between devices  18.5 us (3%)
  between operations  14.4 us (2%)
  other arithmetic  9.25 us (2%)
    psum x2, waiting for transfers between devices, shards(): grad_mixing = lax.psum(lax.psum(grad_local, 'lat'), 'dp') * grad_scale  460 us
    dot_general x5, matrix products, adjoint_rows(): jnp.einsum('kqe,bkqlc->belc', matrix[:, tap_index], grad_filtered, prefer...  29 us
    ppermute x6, starting transfers between devices, shifted(): return lax.ppermute(x, axis, pairs)  18.1 us
  transfers between devices with their start and end apart: 8, of which 3 were waited for; matrix products, arithmetic and copies ran while one was open for 5% of the time, Pallas kernels for 0%

profile of v1, /device:TPU:1, one launch (start us, length us, event | category | flops | bytes accessed | tf_op | source)
XLA Modules:
  0.0 573.0 jit_solution(10104497650867607705)
XLA Ops:
  7.2 0.0 copy-start
  7.2 0.0 copy-start.8
  7.2 0.0 copy-start.2
  7.2 0.0 all-reduce.6.cloned.1.call-start
  7.2 1.3 copy_bitcast_fusion
  8.5 0.2 pad_maximum_fusion
  8.7 7.0 %collective-permute-start = (bf16[2,1,4,128,128]{4,2,3,1,0:T(4,128)(2,1)S(1)}, bf16[2,1,4,128,128]{4,2,3,1,0:T(4,128)(2,1)}, u32[]{:S(2)}, u32[]{:S(2)}) collective-permute-start(bf16[2,1,4,128,128]{4,2,3,1,0:T(4,128)(2,1)S(1)} %pad_maximum_fusion), channel_id=1, source_target_pairs={{0,3},{1,4},{2,5},{3,6},{4,7},{5,8},{6,9},{7,10},{8,11},{9,12},{10... | collective-permute-start | bytes 786440 | tf_op jit(solution)/shard_map/ppermute | solution.py:14
  15.7 3.6 collective-permute-start.1
  19.3 1.9 collective-permute-start.2
  21.2 3.1 collective-permute-start.3
  24.3 1.3 collective-permute-start.4
  25.6 0.8 pad_dynamic-slice_fusion.2
  26.3 0.7 iota_add_fusion
  27.0 0.1 iota_compare_fusion.2
  27.1 5.5 copy.17
  32.6 0.7 dynamic_slice.19
  33.4 0.6 iota_compare_fusion.3
  34.0 2.0 fusion.53
  35.9 0.2 constant_dynamic-slice_fusion
  36.1 0.1 slice_bitcast_fusion.4
  36.2 0.0 collective-permute-done
  36.2 1.3 collective-permute-start.5
  37.5 0.1 dynamic-slice_add_fusion
  37.6 0.7 copy.21
  38.3 0.1 copy.25
  38.4 0.1 copy.19
  38.5 0.1 copy.27
  38.6 0.1 copy.23
  38.8 0.6 copy.31
  39.4 0.1 iota_add_fusion.1
  39.5 0.0 collective-permute-done.1
  39.5 0.0 collective-permute-done.2
  39.5 0.0 collective-permute-done.3
  39.5 0.0 collective-permute-done.4
  39.5 10.8 %collective-permute-done.5 = bf16[2,1,4,128,128]{4,2,3,1,0:T(4,128)(2,1)S(1)} collective-permute-done((bf16[2,1,4,128,128]{4,2,3,1,0:T(4,128)(2,1)S(1)}, bf16[2,1,4,128,128]{4,2,3,1,0:T(4,128)(2,1)S(1)}, u32[]{:S(2)}, u32[]{:S(2)}) %collective-permute-start.5) | collective-permute-done | bytes 262176 | tf_op jit(solution)/shard_map/ppermute | solution.py:14
  50.2 6.7 %concatenate.51 = bf16[2,1,28,128,128]{4,2,3,1,0:T(8,128)(2,1)S(1)} concatenate(bf16[2,1,4,128,128]{4,2,3,1,0:T(4,128)(2,1)} %collective-permute-done, bf16[2,1,4,128,128]{4,2,3,1,0:T(4,128)(2,1)} %collective-permute-done.1, bf16[2,1,4,128,128]{4,2,3,1,0:T(4,128)(2,1)} %collective-permute-done.2, bf16[2,1,4,128,128]{4,2,3,1,0:T(4,128)(2,1)S(1)} %pad_maximum_fusion, ...), dimensions={2} | concatenate | bytes 3670016 | tf_op jit(solution)/shard_map/concatenate | solution.py:52
  57.0 0.4 slice_bitcast_fusion
  57.3 2.3 convert_bitcast_fusion
  59.7 4.5 fusion.20
  64.2 4.4 fusion.32
  68.7 4.6 fusion.23
  73.3 0.3 fusion.87
  73.6 0.3 fusion.89
  73.9 0.0 copy-start.9
  73.9 1.2 fusion.58
  75.1 1.2 fusion.59
  76.3 1.2 bitcast_dynamic-update-slice_fusion
  77.5 1.2 fusion.60
  78.8 1.2 fusion.61
  80.0 3.6 fusion.14
  83.6 2.3 convolution_bitcast_fusion
  85.9 0.0 all-reduce.6.cloned.1.call-update
  85.9 0.0 slice-start
  86.0 0.0 slice-start.3
  86.0 0.0 slice-start.4
  86.0 0.3 all-reduce.8.cloned.1.call-start
  86.3 7.7 %fusion.29 = f32[1,4,128,128]{3,1,2,0:T(4,128)S(1)} fusion(bf16[9,28,128,128]{3,2,0,1:T(8,128)(2,1)} %copy-done.1, bf16[9,28,4]{1,2,0:T(4,128)(2,1)S(1)} %copy.25), kind=kOutput, calls=%fused_computation.23 | convolution fusion | flops 33030144 | bytes 8521696 | tf_op jit(solution)/shard_map/kqe,bkqlc->belc/dot_general | solution.py:58
  94.1 270.8 %all-reduce.6.cloned.1.call-done = f32[9,128,128]{2,1,0:T(8,128)} async-done(((f32[9,128,128]{2,1,0:T(8,128)}), f32[9,128,128]{2,1,0:T(8,128)}) %all-reduce.6.cloned.1.call-update) | async-done | bytes 589840 | tf_op jit(solution)/shard_map/psum | solution.py:111
  364.8 0.0 all-reduce.8.cloned.1.call-update
  364.9 7.8 %fusion.50 = bf16[1,4,128,128]{3,1,2,0:T(4,128)(2,1)S(1)} fusion(bf16[9,28,128,128]{3,2,0,1:T(8,128)(2,1)} %copy-done.1, f32[1,4,2,128]{3,1,2,0:T(4,128)S(1)} %slice-done.1, f32[1,4,126,128]{3,1,2,0:T(4,128)S(1)} %slice-done, f32[1,4,1,128]{3,1,2,0:T(4,128)S(1)} %slice-done.5, f32[1,4,127,128]{3,1,2,0:T(4,128)S(1)} %slice-done.4, ...), kind=kOutput, calls=%fused_computation.31 | convolution fusion | flops 33619968 | bytes 9439200 | tf_op jit(solution)/shard_map/kqe,bkqlc->belc/dot_general | solution.py:58
  372.7 0.7 copy.29
  373.4 1.6 fusion.54
  374.9 189.3 %all-reduce.8.cloned.1.call-done = f32[9,128,128]{2,1,0:T(8,128)} async-done(((f32[9,128,128]{2,1,0:T(8,128)}), f32[9,128,128]{2,1,0:T(8,128)}) %all-reduce.8.cloned.1.call-update) | async-done | bytes 589840 | tf_op jit(solution)/shard_map/psum | solution.py:111
  564.2 1.9 broadcast_multiply_fusion
  (29 shorter events, 0.1 us)
Async XLA Ops:
  7.2 50.2 %copy-start = (bf16[9,128,128]{2,1,0:T(8,128)(2,1)S(1)}, bf16[9,128,128]{2,1,0:T(8,128)(2,1)}, u32[]{:S(2)}) copy-start(bf16[9,128,128]{2,1,0:T(8,128)(2,1)} %param.10) | copy-start | bytes 884740
  7.2 30.3 %copy-start.8 = (s32[128]{0:T(128)S(1)}, s32[128]{0:T(128)}, u32[]{:S(2)}) copy-start(s32[128]{0:T(128)} %param.8) | copy-start | bytes 1540
  7.2 28.7 %copy-start.2 = (bf16[128,25,9,5]{0,1,3,2:T(8,128)(2,1)S(1)}, bf16[128,25,9,5]{0,1,3,2:T(8,128)(2,1)}, u32[]{:S(2)}) copy-start(bf16[128,25,9,5]{0,1,3,2:T(8,128)(2,1)} %param.7) | copy-start | bytes 864004
  7.2 357.6 %all-reduce.6.cloned.1.call-start = ((), (), s32[]{:S(2)}) async-start(), calls=%async_computation | async-start | bytes 1179648 | tf_op jit(solution)/shard_map/psum | solution.py:111
  8.7 27.5 %collective-permute-start = (bf16[2,1,4,128,128]{4,2,3,1,0:T(4,128)(2,1)S(1)}, bf16[2,1,4,128,128]{4,2,3,1,0:T(4,128)(2,1)}, u32[]{:S(2)}, u32[]{:S(2)}) collective-permute-start(bf16[2,1,4,128,128]{4,2,3,1,0:T(4,128)(2,1)S(1)} %pad_maximum_fusion), channel_id=1, source_target_pairs={{0,3},{1,4},{2,5},{3,6},{4,7},{5,8},{6,9},{7,10},{8,11},{9,12},{10... | collective-permute-start | bytes 786440 | tf_op jit(solution)/shard_map/ppermute | solution.py:14
  15.7 23.8 %collective-permute-start.1 = (bf16[2,1,4,128,128]{4,2,3,1,0:T(4,128)(2,1)S(1)}, bf16[2,1,4,128,128]{4,2,3,1,0:T(4,128)(2,1)}, u32[]{:S(2)}, u32[]{:S(2)}) collective-permute-start(bf16[2,1,4,128,128]{4,2,3,1,0:T(4,128)(2,1)S(1)} %pad_maximum_fusion), channel_id=1, source_target_pairs={{0,2},{1,3},{2,4},{3,5},{4,6},{5,7},{6,8},{7,9},{8,10},{9,11},{10,... | collective-permute-start | bytes 786440 | tf_op jit(solution)/shard_map/ppermute | solution.py:14
  19.3 20.2 %collective-permute-start.2 = (bf16[2,1,4,128,128]{4,2,3,1,0:T(4,128)(2,1)S(1)}, bf16[2,1,4,128,128]{4,2,3,1,0:T(4,128)(2,1)}, u32[]{:S(2)}, u32[]{:S(2)}) collective-permute-start(bf16[2,1,4,128,128]{4,2,3,1,0:T(4,128)(2,1)S(1)} %pad_maximum_fusion), channel_id=1, source_target_pairs={{0,1},{1,2},{2,3},{3,4},{4,5},{5,6},{6,7},{7,8},{8,9},{9,10},{10,1... | collective-permute-start | bytes 786440 | tf_op jit(solution)/shard_map/ppermute | solution.py:14
  21.2 18.3 %collective-permute-start.3 = (bf16[2,1,4,128,128]{4,2,3,1,0:T(4,128)(2,1)S(1)}, bf16[2,1,4,128,128]{4,2,3,1,0:T(4,128)(2,1)}, u32[]{:S(2)}, u32[]{:S(2)}) collective-permute-start(bf16[2,1,4,128,128]{4,2,3,1,0:T(4,128)(2,1)S(1)} %pad_maximum_fusion), channel_id=1, source_target_pairs={{1,0},{2,1},{3,2},{4,3},{5,4},{6,5},{7,6},{8,7},{9,8},{10,9},{11,1... | collective-permute-start | bytes 786440 | tf_op jit(solution)/shard_map/ppermute | solution.py:14
  24.3 15.2 %collective-permute-start.4 = (bf16[2,1,4,128,128]{4,2,3,1,0:T(4,128)(2,1)S(1)}, bf16[2,1,4,128,128]{4,2,3,1,0:T(4,128)(2,1)}, u32[]{:S(2)}, u32[]{:S(2)}) collective-permute-start(bf16[2,1,4,128,128]{4,2,3,1,0:T(4,128)(2,1)S(1)} %pad_maximum_fusion), channel_id=1, source_target_pairs={{2,0},{3,1},{4,2},{5,3},{6,4},{7,5},{8,6},{9,7},{10,8},{11,9},{12,... | collective-permute-start | bytes 786440 | tf_op jit(solution)/shard_map/ppermute | solution.py:14
  36.2 14.1 %collective-permute-start.5 = (bf16[2,1,4,128,128]{4,2,3,1,0:T(4,128)(2,1)S(1)}, bf16[2,1,4,128,128]{4,2,3,1,0:T(4,128)(2,1)S(1)}, u32[]{:S(2)}, u32[]{:S(2)}) collective-permute-start(bf16[2,1,4,128,128]{4,2,3,1,0:T(4,128)(2,1)S(1)} %pad_maximum_fusion), channel_id=1, source_target_pairs={{3,0},{4,1},{5,2},{6,3},{7,4},{8,5},{9,6},{10,7},{11,8},{12,9},{13... | collective-permute-start | bytes 786440 | tf_op jit(solution)/shard_map/ppermute | solution.py:14
  59.7 9.0 %copy-start.1 = (bf16[9,28,128,128]{3,2,0,1:T(8,128)(2,1)}, bf16[9,28,128,128]{3,2,0,1:T(8,128)(2,1)S(1)}, u32[]{:S(2)}) copy-start(bf16[9,28,128,128]{3,2,0,1:T(8,128)(2,1)S(1)} %convert_bitcast_fusion) | copy-start | bytes 24772612
  64.2 4.4 copy-start.4
  64.2 4.4 copy-start.7
  68.6 4.6 copy-start.5
  73.3 1.9 copy-start.6
  73.9 6.1 %copy-start.9 = (pred[4,25]{1,0:T(4,128)(4,1)S(1)}, pred[4,25]{1,0:T(4,128)(4,1)}, u32[]{:S(2)}) copy-start(pred[4,25]{1,0:T(4,128)(4,1)} %iota_compare_fusion.3) | copy-start | bytes 304
  78.8 4.8 copy-start.3
  85.9 278.9 %slice-start = ((f32[1,4,128,128]{3,1,2,0:T(4,128)}), f32[1,4,126,128]{3,1,2,0:T(4,128)S(1)}, s32[]{:S(2)}) async-start(f32[1,4,128,128]{3,1,2,0:T(4,128)} %copy-done.4), calls=%async_computation.2 | async-start | bytes 516096 | tf_op jit(solution)/shard_map/jit(_roll_static)/slice | solution.py:64
  85.9 278.9 %slice-start.1 = ((f32[1,4,128,128]{3,1,2,0:T(4,128)}), f32[1,4,2,128]{3,1,2,0:T(4,128)S(1)}, s32[]{:S(2)}) async-start(f32[1,4,128,128]{3,1,2,0:T(4,128)} %copy-done.4), calls=%async_computation.3 | async-start | bytes 8192 | tf_op jit(solution)/shard_map/jit(_roll_static)/slice | solution.py:64
  86.0 278.9 %slice-start.2 = ((f32[1,4,128,128]{3,1,2,0:T(4,128)}), f32[1,4,126,128]{3,1,2,0:T(4,128)S(1)}, s32[]{:S(2)}) async-start(f32[1,4,128,128]{3,1,2,0:T(4,128)} %copy-done.5), calls=%async_computation.4 | async-start | bytes 516096 | tf_op jit(solution)/shard_map/jit(_roll_static)/slice | solution.py:64
  86.0 278.9 %slice-start.3 = ((f32[1,4,128,128]{3,1,2,0:T(4,128)}), f32[1,4,2,128]{3,1,2,0:T(4,128)S(1)}, s32[]{:S(2)}) async-start(f32[1,4,128,128]{3,1,2,0:T(4,128)} %copy-done.5), calls=%async_computation.5 | async-start | bytes 8192 | tf_op jit(solution)/shard_map/jit(_roll_static)/slice | solution.py:64
  86.0 278.9 %slice-start.4 = ((f32[1,4,128,128]{3,1,2,0:T(4,128)}), f32[1,4,127,128]{3,1,2,0:T(4,128)S(1)}, s32[]{:S(2)}) async-start(f32[1,4,128,128]{3,1,2,0:T(4,128)} %copy-done.6), calls=%async_computation.6 | async-start | bytes 520192 | tf_op jit(solution)/shard_map/jit(_roll_static)/slice | solution.py:64
  86.0 278.9 %slice-start.5 = ((f32[1,4,128,128]{3,1,2,0:T(4,128)}), f32[1,4,1,128]{3,1,2,0:T(4,128)S(1)}, s32[]{:S(2)}) async-start(f32[1,4,128,128]{3,1,2,0:T(4,128)} %copy-done.6), calls=%async_computation.7 | async-start | bytes 4096 | tf_op jit(solution)/shard_map/jit(_roll_static)/slice | solution.py:64
  86.0 478.2 %all-reduce.8.cloned.1.call-start = ((), (), s32[]{:S(2)}) async-start(), calls=%async_computation.1 | async-start | bytes 1179648 | tf_op jit(solution)/shard_map/psum | solution.py:111
Sparse Core Ops, SparseCore 0:
  86.1 278.7 all-reduce.5
  368.0 196.1 all-reduce.7
